TPU v7x, 32 devices: a whole 2x2x4 slice. The times are simulated.
32 devices in a mesh: parts: 2 (over x), ctx: 16 (over z, y, core).
Axes of the slice: x: 2, y: 2, z: 4, core: 2. Of those that a mesh axis runs over, the one named last changes fastest.
Arguments:
- queries: bfloat16 [256, 8192], P(('parts', 'ctx')), parts along dimension 0, may hold values from -24 to 24
- steer_ids: int32 [256], P(('parts', 'ctx')), parts along dimension 0, may hold values from 0 to 15
- steer_table: bfloat16 [16, 8192], replicated, may hold values from -3 to 3
- kv: bfloat16 [2, 32768, 1024], P(None, ('parts', 'ctx')), parts along dimension 1, may hold values from -4 to 4
- blocks: int32 [4, 128], P('parts'), parts along dimension 0, may hold values from 0 to 255, as said below
- w_out: bfloat16 [8192, 8192], P('ctx'), may hold values from -0.0625 to 0.0625
Outputs:
- projected: bfloat16 [256, 8192], P(('parts', 'ctx')), parts along dimension 0
There are 2 independent parts, one for each index of `parts`. A program takes and returns all parts, laid end to end along the dimension named above; an argument that names none is the same for every part. Nothing has to cross between parts.
Inputs may be any that keep to these rules, and one draw needn't show every extreme that they name: Each row lists 128 distinct key blocks and always includes block 0 and block 255.
All inputs are finite; a program needn't handle non-finite values.
Results may differ from a plain program's by a relative error of at most 0.0066.
Values may be sent and summed in bfloat16 or wider, within the bound.
A program may use at most 64 MiB of HBM per device.

v0:
```python
import jax
import jax.numpy as jnp
from jax import lax
from jax.sharding import PartitionSpec as P

HEADS = 64
KV_HEADS = 8
HEAD = 128
D = 8192
BLOCK = 64


def apply_steer(queries, steer_ids, steer_table):
    lookup_ids = jnp.arange(steer_table.shape[0], dtype=jnp.int32)
    one_hot = (steer_ids[:, None] == lookup_ids[None, :]).astype(jnp.bfloat16)
    lookup = jnp.dot(one_hot, steer_table, preferred_element_type=jnp.float32)
    return (queries.astype(jnp.float32) + lookup).astype(jnp.bfloat16)


def local_keep(blocks, first_block, block_count, query_count):
    block_ids = first_block + jnp.arange(block_count, dtype=jnp.int32)
    hits = jnp.any(blocks[:, :, None] == block_ids[None, None, :], axis=1)
    full = jnp.broadcast_to(
        hits[:, None, :, None], (query_count // BLOCK, BLOCK, block_count, BLOCK)
    )
    return full.reshape(query_count, block_count * BLOCK)


def group_attend(q_rows, k_rows, v_rows, keep_rows):
    scores = lax.dot_general(
        q_rows, k_rows, (((1,), (1,)), ((), ())), preferred_element_type=jnp.float32
    )
    scores = scores * HEAD ** (-0.5)
    masked = jnp.where(keep_rows, scores, jnp.float32(-1e30))
    row_peak = jnp.max(masked, axis=1)
    weights = jnp.where(keep_rows, jnp.exp(masked - row_peak[:, None]), jnp.float32(0.0))
    row_total = jnp.sum(weights, axis=1)
    probs = weights.astype(jnp.bfloat16)
    partial_out = jnp.dot(probs, v_rows, preferred_element_type=jnp.float32)
    return (row_peak, row_total, partial_out)


def partial_attention(steered, kv_piece, keep_mask):
    query_count = steered.shape[0]
    ctx_count = kv_piece.shape[1]
    group_size = HEADS // KV_HEADS
    q_groups = steered.reshape(query_count, KV_HEADS, group_size, HEAD).transpose(1, 2, 0, 3)
    q_groups = q_groups.reshape(KV_HEADS, group_size * query_count, HEAD)
    k_groups = kv_piece[0].reshape(ctx_count, KV_HEADS, HEAD).transpose(1, 0, 2)
    v_groups = kv_piece[1].reshape(ctx_count, KV_HEADS, HEAD).transpose(1, 0, 2)
    keep_rows = jnp.tile(keep_mask, (group_size, 1))

    def one_group(triple):
        return group_attend(triple[0], triple[1], triple[2], keep_rows)

    peaks, totals, outs = lax.map(one_group, (q_groups, k_groups, v_groups))
    peaks = (
        peaks.reshape(KV_HEADS, group_size, query_count)
        .transpose(2, 0, 1)
        .reshape(query_count, HEADS)
    )
    totals = (
        totals.reshape(KV_HEADS, group_size, query_count)
        .transpose(2, 0, 1)
        .reshape(query_count, HEADS)
    )
    outs = (
        outs.reshape(KV_HEADS, group_size, query_count, HEAD)
        .transpose(2, 0, 1, 3)
        .reshape(query_count, HEADS * HEAD)
    )
    return (peaks, totals, outs)


def per_device(queries, steer_ids, steer_table, kv, blocks, w_out):
    steered_local = apply_steer(queries, steer_ids, steer_table)
    steered = lax.all_gather(steered_local, "ctx", axis=0, tiled=True)
    shard_count = lax.axis_size("ctx")
    my_index = lax.axis_index("ctx")
    query_count = steered.shape[0]
    block_count = kv.shape[1] // BLOCK
    keep_mask = local_keep(blocks, my_index * block_count, block_count, query_count)
    peaks, totals, outs = partial_attention(steered, kv, keep_mask)
    stat_width = max(HEADS, shard_count)
    per_entry = D // stat_width
    col_count = D // shard_count

    def spread(values):
        return jnp.repeat(values, stat_width // HEADS, axis=1)

    got_num, got_max, got_den = (
        lax.all_to_all(outs, "ctx", split_axis=1, concat_axis=0, tiled=True),
        lax.all_to_all(spread(peaks), "ctx", split_axis=1, concat_axis=0, tiled=True),
        lax.all_to_all(spread(totals), "ctx", split_axis=1, concat_axis=0, tiled=True),
    )
    got_num = got_num.reshape(shard_count, query_count, col_count)
    got_max = got_max.reshape(shard_count, query_count, stat_width // shard_count)
    got_den = got_den.reshape(shard_count, query_count, stat_width // shard_count)
    overall = jnp.max(got_max, axis=0)
    scales = jnp.exp(got_max - overall[None])
    denominator = jnp.sum(scales * got_den, axis=0)
    numerator = jnp.sum(jnp.repeat(scales, per_entry, axis=2) * got_num, axis=0)
    attended = (numerator / jnp.repeat(denominator, per_entry, axis=1)).astype(jnp.bfloat16)
    return lax.psum_scatter(
        jnp.dot(attended, w_out, preferred_element_type=jnp.float32),
        "ctx",
        scatter_dimension=0,
        tiled=True,
    ).astype(jnp.bfloat16)


def solution(mesh):
    return jax.shard_map(
        per_device,
        mesh=mesh,
        in_specs=(
            P(("parts", "ctx"), None),
            P(("parts", "ctx")),
            P(),
            P(None, ("parts", "ctx"), None),
            P("parts", None),
            P("ctx", None),
        ),
        out_specs=P(("parts", "ctx"), None),
        check_vma=False,
    )
```

profile of v0, /device:TPU:0, one launch (start us, length us, event | category | flops | bytes accessed | tf_op | source)
XLA Modules:
  0.0 324.1 jit_solution(4779056116548888666)
XLA Ops:
  6.5 0.9 copy-done
  7.5 1.8 fusion.25
  9.3 4.0 %fusion.32 = (bf16[1,1024,1024]{2,1,0:T(8,128)(2,1)S(1)}, bf16[1,1024,1024]{2,1,0:T(8,128)(2,1)}) fusion(bf16[2,1024,1024]{2,1,0:T(8,128)(2,1)} %param.11), kind=kLoop, calls=%fused_computation.38 | loop fusion | bytes 8388608 | tf_op jit(solution)/shard_map/slice | solution.py:50
  13.4 4.0 %copy.38 = bf16[1,1024,1024]{1,2,0:T(8,128)(2,1)} copy(bf16[1,1024,1024]{2,1,0:T(8,128)(2,1)} %get-tuple-element.124) | data formatting | bytes 4194304
  17.3 2.6 copy.39
  20.9 32.7 %all-gather.2.cloned.1.call-done = bf16[128,8192]{1,0:T(8,128)(2,1)} async-done(((bf16[8,8192]{1,0:T(8,128)(2,1)}), bf16[128,8192]{1,0:T(8,128)(2,1)}) %all-gather.2.cloned.1.call-update) | async-done | bytes 2097168 | tf_op jit(solution)/shard_map/all_gather | solution.py:77
  53.7 2.2 copy.41
  55.8 1.4 copy.29
  57.2 58.5 %while.15 = (s32[]{:T(128)}, f32[8,1024]{1,0:T(8,128)S(1)}, f32[8,1024]{1,0:T(8,128)S(1)}, f32[8,1024,128]{2,1,0:T(8,128)}, bf16[8,1024,128]{2,1,0:T(8,128)(2,1)...) while((s32[]{:T(128)}, f32[8,1024]{1,0:T(8,128)S(1)}, ...), condition=%wide.region_4.5_spmd.clone, body=%wide.region_1.4_spmd.clone.sunk | while | flops 550500352 | bytes 18253932 | solution.py:56
  57.2 0.5 tile.22
  57.7 2.0 fusion.44
  59.8 3.2 fusion.46
  63.0 1.3 fusion.45
  64.5 0.5 tile.22
  65.0 2.0 fusion.44
  67.1 3.2 fusion.46
  70.3 1.3 fusion.45
  72.3 2.0 fusion.44
  74.4 3.2 fusion.46
  77.6 1.3 fusion.45
  79.6 2.0 fusion.44
  81.7 3.2 fusion.46
  84.9 1.3 fusion.45
  87.0 2.0 fusion.44
  89.0 3.2 fusion.46
  92.2 1.3 fusion.45
  94.3 2.0 fusion.44
  96.3 3.2 fusion.46
  99.5 1.3 fusion.45
  101.6 2.0 fusion.44
  103.6 3.2 fusion.46
  106.8 1.3 fusion.45
  108.9 2.0 fusion.44
  110.9 3.2 fusion.46
  114.2 1.3 fusion.45
  115.7 0.6 copy.58
  116.3 3.5 %all-to-all-start = ((f32[128,16,4]{0,2,1:T(4,128)}), f32[128,16,4]{0,2,1:T(4,128)S(1)}, u32[]{:S(2)}, u32[]{:S(2)}) async-start(f32[128,16,4]{0,2,1:T(4,128)} %bitcast.7), calls=%async_computation | async-start | bytes 65536 | tf_op jit(solution)/shard_map/all_to_all | solution.py:93
  119.8 0.6 copy.57
  120.4 6.0 %all-to-all-done = f32[128,16,4]{0,2,1:T(4,128)S(1)} async-done(((f32[128,16,4]{0,2,1:T(4,128)}), f32[128,16,4]{0,2,1:T(4,128)S(1)}, u32[]{:S(2)}, u32[]{:S(2)}) %all-to-all-start) | async-done | bytes 32800 | tf_op jit(solution)/shard_map/all_to_all | solution.py:93
  126.4 3.5 %all-to-all-start.2 = ((f32[128,16,4]{0,2,1:T(4,128)}), f32[128,16,4]{0,2,1:T(4,128)S(1)}, u32[]{:S(2)}, u32[]{:S(2)}) async-start(f32[128,16,4]{0,2,1:T(4,128)} %bitcast.15), calls=%async_computation.2 | async-start | bytes 65536 | tf_op jit(solution)/shard_map/all_to_all | solution.py:94
  129.9 5.4 %copy.35 = f32[128,8,8,128]{0,3,2,1:T(8,128)} copy(f32[128,8,8,128]{3,0,2,1:T(8,128)} %bitcast.11) | data formatting | bytes 8388608 | tf_op jit(solution)/shard_map/transpose | solution.py:69
  135.3 1.2 all-to-all-done.2
  136.5 4.8 %all-to-all-start.1 = ((f32[128,16,512]{0,2,1:T(8,128)}), f32[128,16,512]{0,2,1:T(8,128)}, u32[]{:S(2)}, u32[]{:S(2)}) async-start(f32[128,16,512]{0,2,1:T(8,128)} %bitcast.118), calls=%async_computation.1 | async-start | bytes 8388608 | tf_op jit(solution)/shard_map/all_to_all | solution.py:92
  141.4 77.6 %all-to-all-done.1 = f32[128,16,512]{0,2,1:T(8,128)} async-done(((f32[128,16,512]{0,2,1:T(8,128)}), f32[128,16,512]{0,2,1:T(8,128)}, u32[]{:S(2)}, u32[]{:S(2)}) %all-to-all-start.1) | async-done | bytes 4194336 | tf_op jit(solution)/shard_map/all_to_all | solution.py:92
  219.0 2.5 fusion.26
  221.6 6.6 %fusion.33 = f32[128,8192]{1,0:T(8,128)} fusion(bf16[128,512]{0,1:T(8,128)(2,1)S(1)} %fusion.27, bf16[512,8192]{1,0:T(8,128)(2,1)} %param.13), kind=kOutput, calls=%fused_computation.39 | convolution fusion | flops 1073741824 | bytes 12713984 | tf_op jit(solution)/shard_map/dot_general | solution.py:105
  228.2 87.5 %reduce-scatter.2.cloned.1.call-done = f32[8,8192]{1,0:T(8,128)} async-done(((f32[128,8192]{1,0:T(8,128)}), f32[8,8192]{1,0:T(8,128)}) %reduce-scatter.2.cloned.1.call-update) | async-done | bytes 262160 | tf_op jit(solution)/shard_map/reduce_scatter | solution.py:104
  315.7 1.6 convert_element_type.19
  (40 shorter events, 5.8 us)
Async XLA Ops:
  6.5 1.0 copy-start
  6.5 47.1 %all-gather.2.cloned.1.call-start = ((), (), s32[]{:S(2)}) async-start(), calls=%async_computation.4 | async-start | bytes 2228224 | tf_op jit(solution)/shard_map/all_gather | solution.py:77
  13.4 6.5 %copy-start.1 = (s32[2,128]{1,0:T(2,128)S(1)}, s32[2,128]{1,0:T(2,128)}, u32[]{:S(2)}) copy-start(s32[2,128]{1,0:T(2,128)} %param.12) | copy-start | bytes 3076
  116.3 10.1 %all-to-all-start = ((f32[128,16,4]{0,2,1:T(4,128)}), f32[128,16,4]{0,2,1:T(4,128)S(1)}, u32[]{:S(2)}, u32[]{:S(2)}) async-start(f32[128,16,4]{0,2,1:T(4,128)} %bitcast.7), calls=%async_computation | async-start | bytes 65536 | tf_op jit(solution)/shard_map/all_to_all | solution.py:93
  126.4 10.1 %all-to-all-start.2 = ((f32[128,16,4]{0,2,1:T(4,128)}), f32[128,16,4]{0,2,1:T(4,128)S(1)}, u32[]{:S(2)}, u32[]{:S(2)}) async-start(f32[128,16,4]{0,2,1:T(4,128)} %bitcast.15), calls=%async_computation.2 | async-start | bytes 65536 | tf_op jit(solution)/shard_map/all_to_all | solution.py:94
  136.5 82.5 %all-to-all-start.1 = ((f32[128,16,512]{0,2,1:T(8,128)}), f32[128,16,512]{0,2,1:T(8,128)}, u32[]{:S(2)}, u32[]{:S(2)}) async-start(f32[128,16,512]{0,2,1:T(8,128)} %bitcast.118), calls=%async_computation.1 | async-start | bytes 8388608 | tf_op jit(solution)/shard_map/all_to_all | solution.py:92
  141.3 174.4 %reduce-scatter.2.cloned.1.call-start = ((), (), s32[]{:S(2)}) async-start(), calls=%async_computation.5 | async-start | bytes 4456448 | tf_op jit(solution)/shard_map/reduce_scatter | solution.py:104
Sparse Core Ops, SparseCore 0:
  9.5 44.0 all-gather.1
  228.3 87.2 reduce-scatter.1
where the time goes:
time: 325 us; the launch traced here: 324 us
  waiting for transfers between devices  205 us (63%)
  matrix products  50.6 us (16%)
  local copies, waits for them, and re-layouts  28 us (9%)
  other arithmetic  14.8 us (5%)
  between operations  13.5 us (4%)
  starting transfers between devices  11.8 us (4%)
    reduce_scatter x1, waiting for transfers between devices, per_device(): lax.psum_scatter(jnp.dot(attended, w_out, preferred_element_type=jnp.floa...  87.5 us
    all_to_all x1, waiting for transfers between devices, per_device(): lax.all_to_all(outs, 'ctx', split_axis=1, concat_axis=0, tiled=True)  77.6 us
    all_gather x1, waiting for transfers between devices, per_device(): steered = lax.all_gather(steered_local, 'ctx', axis=0, tiled=True)  32.7 us
    dot_general x8, matrix products, group_attend(): partial_out = jnp.dot(probs, v_rows, preferred_element_type=jnp.float32)  25.8 us
    dot_general x8, matrix products, group_attend(): lax.dot_general(q_rows, k_rows, (((1,), (1,)), ((), ())), preferred_eleme...  16.4 us
    unnamed x10, local copies, waits for them, and re-layouts  11.2 us
    reduce_sum x8, other arithmetic, group_attend(): row_total = jnp.sum(weights, axis=1)  10.4 us
    dot_general x1, matrix products, per_device(): jnp.dot(attended, w_out, preferred_element_type=jnp.float32)  6.63 us
  transfers between devices with their start and end apart: 5, of which 5 were waited for; matrix products, arithmetic and copies ran while one was open for 5% of the time, Pallas kernels for 0%

commit v1 on v0

--- a/solution.py
+++ b/solution.py
@@ -1,6 +1,8 @@
 import jax
 import jax.numpy as jnp
 from jax import lax
+from jax.experimental import pallas as pl
+from jax.experimental.pallas import tpu as pltpu
 from jax.sharding import PartitionSpec as P
 
 HEADS = 64
@@ -109,9 +111,323 @@
     ).astype(jnp.bfloat16)
 
 
+MESH = pl.DeviceIdType.MESH
+EXP_SCALE = HEAD ** (-0.5) * 1.4426950408889634
+GROUP = HEADS // KV_HEADS
+OWN = GROUP // 2
+CHUNKS = 4
+CHUNK_COLS = D // CHUNKS
+TILE = CHUNK_COLS // 2
+
+
+def fused_kernel(
+    q_ref, ids_ref, table_ref, blocks_ref, kv_hbm, w_hbm, out_ref,
+    kv_ref, w_ref, q_all, bias_ref, q_rows, v_t,
+    o_loc, s_loc, r1, rs1, t1, ts1, r2, rs2, t2, ts2, r3, rs3, t3, ts3, r4, rs4,
+    att, p0, pr1, p1, pr2, p2, pr3, p3, pr4,
+    kv_sem, w_sem, ag_send, ag_recv, rs_send, rs_recv, ss_send, ss_recv, pj_send, pj_recv,
+):
+    me = lax.axis_index("ctx")
+    core = me % 2
+    y = (me // 2) % 2
+    z0 = (me // 4) % 2
+    z1 = me // 8
+    to_core = me + 1 - 2 * core
+    to_y = me + 2 - 4 * y
+    to_z0 = me + 4 - 8 * z0
+    to_z1 = me + 8 - 16 * z1
+    groups = q_all.shape[0]
+    rows = q_ref.shape[0]
+    keys = kv_ref.shape[1]
+    key_blocks = keys // BLOCK
+    queries = rows * 2 * groups
+
+    kv_load = pltpu.make_async_copy(kv_hbm, kv_ref, kv_sem)
+    w_load = pltpu.make_async_copy(w_hbm, w_ref, w_sem)
+    kv_load.start()
+    w_load.start()
+
+    barrier = pltpu.get_barrier_semaphore()
+    for other in (to_core, to_y, to_z0, to_z1):
+        pl.semaphore_signal(barrier, inc=1, device_id={"ctx": other}, device_id_type=MESH)
+
+    lookup_ids = lax.broadcasted_iota(jnp.int32, (rows, table_ref.shape[0]), 1)
+    one_hot = jnp.where(ids_ref[...] == lookup_ids, 1.0, 0.0).astype(jnp.bfloat16)
+    for g in range(groups):
+        cols = slice(g * GROUP * HEAD, (g + 1) * GROUP * HEAD)
+        lookup = jnp.dot(one_hot, table_ref[:, cols], preferred_element_type=jnp.float32)
+        steered = q_ref[:, cols].astype(jnp.float32) + lookup
+        stacked = jnp.concatenate(
+            [steered[:, h * HEAD:(h + 1) * HEAD] for h in range(GROUP)], axis=0
+        )
+        q_all[g, z1, z0, y, core] = stacked.astype(jnp.bfloat16)
+
+    def remote(src, dst, send, recv, other):
+        return pltpu.make_async_remote_copy(
+            src_ref=src, dst_ref=dst, send_sem=send, recv_sem=recv,
+            device_id={"ctx": other}, device_id_type=MESH,
+        )
+
+    def gather(step, g):
+        if step == 0:
+            ref, other = q_all.at[g, z1, z0, y, core], to_z1
+        elif step == 1:
+            ref, other = q_all.at[g, :, z0, y, core], to_z0
+        elif step == 2:
+            ref, other = q_all.at[g, :, :, y, core], to_y
+        else:
+            ref, other = q_all.at[g, :, :, :, core], to_core
+        return remote(ref, ref, ag_send.at[step, g], ag_recv.at[step, g], other)
+
+    def merge_copies(step, i):
+        if step == 0:
+            a, b = (o_loc.at[i, 1 - core], r1.at[i]), (s_loc.at[i, 1 - core], rs1.at[i])
+            other = to_core
+        elif step == 1:
+            a, b = (t1.at[2 * i + 1 - y], r2.at[i]), (ts1.at[2 * i + 1 - y], rs2.at[i])
+            other = to_y
+        elif step == 2:
+            a, b = (t2.at[2 * i + 1 - z0], r3.at[i]), (ts2.at[2 * i + 1 - z0], rs3.at[i])
+            other = to_z0
+        else:
+            a, b = (t3.at[1 - z1], r4.at[i]), (ts3.at[1 - z1], rs4.at[i])
+            other = to_z1
+        return (
+            remote(a[0], a[1], rs_send.at[step, i], rs_recv.at[step, i], other),
+            remote(b[0], b[1], ss_send.at[step, i], ss_recv.at[step, i], other),
+        )
+
+    def start_merge(step, i):
+        for copy in merge_copies(step, i):
+            copy.start()
+
+    def wait_merge(step, i):
+        for copy in merge_copies(step, i):
+            copy.wait_recv()
+
+    def merge_stats(sa, sb):
+        ma, mb = sa[:OWN], sb[:OWN]
+        peak = jnp.maximum(ma, mb)
+        wa = jnp.exp2((ma - peak) * EXP_SCALE)
+        wb = jnp.exp2((mb - peak) * EXP_SCALE)
+        return peak, wa, wb, wa * sa[OWN:] + wb * sb[OWN:]
+
+    def merge(oa, sa, ob, sb, o_dst, s_dst):
+        peak, wa, wb, total = merge_stats(sa[...], sb[...])
+        s_dst[...] = jnp.concatenate([peak, total], axis=0)
+        for h in range(OWN):
+            o_dst[h] = (
+                oa[h].astype(jnp.float32) * wa[h:h + 1]
+                + ob[h].astype(jnp.float32) * wb[h:h + 1]
+            ).astype(jnp.bfloat16)
+
+    first = me * key_blocks
+    block_ids = first + lax.broadcasted_iota(jnp.int32, (key_blocks, blocks_ref.shape[1]), 0)
+    lane_block = (lax.broadcasted_iota(jnp.int32, (key_blocks, 2 * queries), 1) % queries) // BLOCK
+    bias = jnp.zeros((key_blocks, 2 * queries), jnp.float32)
+    for b in range(blocks_ref.shape[0]):
+        same = jnp.where(block_ids == blocks_ref[b:b + 1, :], 1.0, 0.0)
+        hit = jnp.max(same, axis=1, keepdims=True)
+        bias = jnp.where(lane_block == b, (hit - 1.0) * 1e30, bias)
+    bias_ref[...] = bias
+
+    pl.semaphore_wait(barrier, 4)
+
+    @pl.loop(0, groups)
+    def _(g):
+        gather(0, g).start()
+
+    kv_load.wait()
+
+    def attend(g):
+        lanes = pl.ds(pl.multiple_of(g * HEAD, HEAD), HEAD)
+        v_t[...] = kv_ref[1, :, lanes].T
+        q_wide = q_all[g].reshape(2 * groups, GROUP * rows, HEAD).astype(jnp.float32)
+        for h in range(GROUP):
+            head_rows = q_wide[:, h * rows:(h + 1) * rows, :].reshape(queries, HEAD)
+            q_rows[h // 2, (h % 2) * queries:(h % 2 + 1) * queries] = head_rows.astype(jnp.bfloat16)
+
+        @pl.loop(0, GROUP // 2)
+        def _(hp):
+            scores = lax.dot_general(
+                kv_ref[0, :, lanes], q_rows[hp], (((1,), (1,)), ((), ())),
+                preferred_element_type=jnp.float32,
+            )
+            scores = scores.reshape(key_blocks, BLOCK, 2 * queries) + bias_ref[...][:, None, :]
+            scores = scores.reshape(keys, 2 * queries)
+            peak = jnp.max(scores, axis=0, keepdims=True)
+            weights = jnp.exp2((scores - peak) * EXP_SCALE)
+            total = jnp.sum(weights, axis=0, keepdims=True)
+            part = jnp.dot(v_t[...], weights.astype(jnp.bfloat16), preferred_element_type=jnp.float32)
+            half = hp // (OWN // 2)
+            base = (hp % (OWN // 2)) * 2
+            for i in range(2):
+                lane = slice(i * queries, (i + 1) * queries)
+                o_loc[g, half, base + i] = part[:, lane].astype(jnp.bfloat16)
+                s_loc[g, half, pl.ds(base + i, 1), :] = peak[:, lane]
+                s_loc[g, half, pl.ds(OWN + base + i, 1), :] = total[:, lane]
+
+    def at(cond, fn):
+        pl.when(cond)(fn)
+
+    @pl.loop(0, groups + 6)
+    def _(t):
+        for step in range(3):
+            def advance(step=step):
+                gather(step, t - step).wait_recv()
+                gather(step + 1, t - step).start()
+            at((t >= step) & (t < groups + step), advance)
+
+        def attention():
+            g = t - 3
+            gather(3, g).wait_recv()
+            attend(g)
+            start_merge(0, g)
+        at((t >= 3) & (t < groups + 3), attention)
+
+        def merge_core():
+            g = t - 4
+            wait_merge(0, g)
+            merge(o_loc.at[g, core], s_loc.at[g, core], r1.at[g], rs1.at[g], t1.at[g], ts1.at[g])
+            at(g % 2 == 1, lambda: start_merge(1, g // 2))
+        at((t >= 4) & (t < groups + 4), merge_core)
+
+        def merge_y():
+            j = (t - 5) // 2
+            wait_merge(1, j)
+            merge(t1.at[2 * j + y], ts1.at[2 * j + y], r2.at[j], rs2.at[j], t2.at[j], ts2.at[j])
+            at(j % 2 == 1, lambda: start_merge(2, j // 2))
+        at((t >= 6) & (t < groups + 5) & (t % 2 == 0), merge_y)
+
+        def merge_z0():
+            k = (t - 6) // 4
+            wait_merge(2, k)
+            merge(t2.at[2 * k + z0], ts2.at[2 * k + z0], r3.at[k], rs3.at[k], t3.at[k], ts3.at[k])
+        at((t >= 9) & (t < groups + 6) & (t % 4 == 1), merge_z0)
+
+    start_merge(3, 0)
+    w_load.wait()
+    wait_merge(3, 0)
+    peak, wa, wb, total = merge_stats(ts3[z1], rs4[0])
+    inverse = 1.0 / total
+    wa, wb = wa * inverse, wb * inverse
+    for h in range(OWN):
+        done = t3[z1, h].astype(jnp.float32) * wa[h:h + 1] + r4[0, h].astype(jnp.float32) * wb[h:h + 1]
+        att[:, h * HEAD:(h + 1) * HEAD] = done.T.astype(jnp.bfloat16)
+
+    def project_copy(step, c):
+        swap = c % 2 == 1
+        if step == 0:
+            src, dst, other = p0.at[c, :, :, :, 1 - core], pr1.at[c], to_core
+        elif step == 1:
+            src = p1.at[c, :, 1 - z0] if swap else p1.at[c, :, :, 1 - y]
+            dst, other = pr2.at[c], to_z0 if swap else to_y
+        elif step == 2:
+            src = p2.at[c, :, 1 - y] if swap else p2.at[c, :, 1 - z0]
+            dst, other = pr3.at[c], to_y if swap else to_z0
+        else:
+            src, dst, other = p3.at[c, 1 - z1], pr4.at[c], to_z1
+        return remote(src, dst, pj_send.at[step, c], pj_recv.at[step, c], other)
+
+    def add(a, b):
+        return (a.astype(jnp.float32) + b.astype(jnp.float32)).astype(jnp.bfloat16)
+
+    def stage(step, c):
+        swap = c % 2 == 1
+        if step == 0:
+            halves = []
+            for i in range(2):
+                base = c * CHUNK_COLS + i * TILE
+                part = jnp.dot(att[...], w_ref[:, base:base + TILE], preferred_element_type=jnp.float32)
+                halves.append(part.reshape(2 * groups, rows, TILE))
+            both = jnp.concatenate(halves, axis=1).astype(jnp.bfloat16)
+            p0[c] = both.reshape(2, 2, 2, 2, 2 * rows, TILE)
+        else:
+            project_copy(step - 1, c).wait_recv()
+            if step == 1:
+                p1[c] = add(p0[c, :, :, :, core], pr1[c])
+            elif step == 2:
+                p2[c] = add(p1[c, :, z0] if swap else p1[c, :, :, y], pr2[c])
+            elif step == 3:
+                p3[c] = add(p2[c, :, y] if swap else p2[c, :, z0], pr3[c])
+            else:
+                done = p3[c, z1].astype(jnp.float32) + pr4[c].astype(jnp.float32)
+                for i in range(2):
+                    base = c * CHUNK_COLS + i * TILE
+                    out_ref[:, base:base + TILE] = done[i * rows:(i + 1) * rows].astype(jnp.bfloat16)
+        if step < 4:
+            project_copy(step, c).start()
+
+    for t in range(CHUNKS + 4):
+        for step in range(5):
+            if 0 <= t - step < CHUNKS:
+                stage(step, t - step)
+
+    @pl.loop(0, groups)
+    def _(g):
+        for step in range(4):
+            gather(step, g).wait_send()
+
+    for step in range(4):
+        for i in range(groups >> step):
+            for copy in merge_copies(step, i):
+                copy.wait_send()
+        for c in range(CHUNKS):
+            project_copy(step, c).wait_send()
+
+
+def per_device_fused(queries, steer_ids, steer_table, kv, blocks, w_out):
+    rows = queries.shape[0]
+    keys = kv.shape[1]
+    groups = KV_HEADS
+    total_q = 2 * groups * rows
+    bf, f32 = jnp.bfloat16, jnp.float32
+    piece = (OWN, HEAD, total_q)
+    stat = (2 * OWN, total_q)
+    tile = (2 * rows, TILE)
+    scratch = [
+        pltpu.VMEM(kv.shape, bf),
+        pltpu.VMEM(w_out.shape, bf),
+        pltpu.VMEM((groups, 2, 2, 2, 2, GROUP * rows, HEAD), bf),
+        pltpu.VMEM((keys // BLOCK, 2 * total_q), f32),
+        pltpu.VMEM((GROUP // 2, 2 * total_q, HEAD), bf),
+        pltpu.VMEM((HEAD, keys), bf),
+        pltpu.VMEM((groups, 2) + piece, bf),
+        pltpu.VMEM((groups, 2) + stat, f32),
+    ]
+    for count in (groups, groups // 2, groups // 4):
+        scratch += [
+            pltpu.VMEM((count,) + piece, bf), pltpu.VMEM((count,) + stat, f32),
+            pltpu.VMEM((count,) + piece, bf), pltpu.VMEM((count,) + stat, f32),
+        ]
+    scratch += [pltpu.VMEM((1,) + piece, bf), pltpu.VMEM((1,) + stat, f32)]
+    scratch += [
+        pltpu.VMEM((total_q, OWN * HEAD), bf),
+        pltpu.VMEM((CHUNKS, 2, 2, 2, 2) + tile, bf),
+    ]
+    for lead in ((2, 2, 2), (2, 2), (2,)):
+        scratch += [pltpu.VMEM((CHUNKS,) + lead + tile, bf), pltpu.VMEM((CHUNKS,) + lead + tile, bf)]
+    scratch += [pltpu.VMEM((CHUNKS,) + tile, bf)]
+    dma = pltpu.SemaphoreType.DMA
+    scratch += [dma(()), dma(())] + [dma((4, groups))] * 6 + [dma((4, CHUNKS))] * 2
+    vmem = pl.BlockSpec(memory_space=pltpu.VMEM)
+    hbm = pl.BlockSpec(memory_space=pl.ANY)
+    return pl.pallas_call(
+        fused_kernel,
+        out_shape=jax.ShapeDtypeStruct(queries.shape, bf),
+        in_specs=[vmem, vmem, vmem, vmem, hbm, hbm],
+        out_specs=vmem,
+        scratch_shapes=scratch,
+        compiler_params=pltpu.CompilerParams(
+            collective_id=0, has_side_effects=True, vmem_limit_bytes=48 * 1024 * 1024
+        ),
+    )(queries, steer_ids[:, None], steer_table, blocks, kv, w_out)
+
+
 def solution(mesh):
+    fits = mesh.shape["ctx"] == 2 * KV_HEADS
     return jax.shard_map(
-        per_device,
+        per_device_fused if fits else per_device,
         mesh=mesh,
         in_specs=(
             P(("parts", "ctx"), None),

time: 325 us -> 97.9 us (0.30)
  waiting for transfers between devices: 205 us -> 0 us
  Pallas kernels: 0 us -> 91.2 us
  matrix products: 50.6 us -> 0 us
  local copies, waits for them, and re-layouts: 28 us -> 6.11 us
  other arithmetic: 14.8 us -> 0 us
  between operations: 13.5 us -> 0.01 us
  starting transfers between devices: 11.8 us -> 0 us
    pallas_call x0 -> x1, Pallas kernels: none -> 91.2 us  [per_device_fused(): pl.pallas_call(fused_kernel, out_shape=jax.ShapeDtypeStruct(queries.shape...]
    reduce_scatter x1 -> x0, waiting for transfers between devices: 87.5 us -> none  [per_device(): lax.psum_scatter(jnp.dot(attended, w_out, preferred_element_type=jnp.floa...]
    all_to_all x3 -> x0, waiting for transfers between devices: 84.8 us -> none  [the longest x1 77.6 us: per_device(): lax.all_to_all(outs, 'ctx', split_axis=1, concat_axis=0, tiled=True)]
    dot_general x18 -> x0, matrix products: 50.6 us -> none  [the longest x8 25.8 us: group_attend(): partial_out = jnp.dot(probs, v_rows, preferred_element_type=jnp.float32)]
    all_gather x1 -> x0, waiting for transfers between devices: 32.7 us -> none  [per_device(): steered = lax.all_gather(steered_local, 'ctx', axis=0, tiled=True)]
    reduce_sum x10 -> x0, other arithmetic: 13 us -> none  [the longest x8 10.4 us: group_attend(): row_total = jnp.sum(weights, axis=1)]
    all_to_all x3 -> x0, starting transfers between devices: 11.8 us -> none  [the longest x1 4.78 us: per_device(): lax.all_to_all(outs, 'ctx', split_axis=1, concat_axis=0, tiled=True)]
    transpose x2 -> x0, local copies, waits for them, and re-layouts: 6.71 us -> none  [the longest x1 5.35 us: partial_attention(): outs = outs.reshape(KV_HEADS, group_size, query_count, HEAD).transpose(2,...]
  transfers between devices with their start and end apart: 5 -> 0, of which waited for: 5 -> 0; matrix products, arithmetic and copies ran while one was open for 5% -> 0% of each run, Pallas kernels for 0% -> 0%
where the time goes in v1:
time: 97.9 us; the launch traced here: 97.3 us
  Pallas kernels  91.2 us (93%)
  local copies, waits for them, and re-layouts  6.11 us (6%)
    pallas_call x1, Pallas kernels, per_device_fused(): pl.pallas_call(fused_kernel, out_shape=jax.ShapeDtypeStruct(queries.shape...  91.2 us
    unnamed x9, local copies, waits for them, and re-layouts  5.38 us

profile of v1, /device:TPU:0, one launch (start us, length us, event | category | flops | bytes accessed | tf_op | source)
XLA Modules:
  0.0 97.3 jit_solution(18431197396495915170)
XLA Ops:
  0.0 0.7 copy.7.ids_ref
  0.7 0.0 copy-start
  0.7 2.2 %copy-done = bf16[2,1024,1024]{2,1,0:T(8,128)(2,1)S(1)} copy-done((bf16[2,1024,1024]{2,1,0:T(8,128)(2,1)S(1)}, bf16[2,1024,1024]{2,1,0:T(8,128)(2,1)}, u32[]{:S(2)}) %copy-start) | copy-done | bytes 4194328
  2.9 0.0 copy-start.1
  2.9 0.9 copy-done.1
  3.9 0.0 copy-start.2
  3.9 0.9 copy-done.2
  4.8 0.0 copy-start.3
  4.8 0.7 copy-done.3
  5.5 91.2 %shard_map.64 = bf16[8,8192]{1,0:T(8,128)(2,1)S(1)} custom-call(bf16[8,8192]{1,0:T(8,128)(2,1)S(1)} %copy-done.2, s32[8,1]{1,0:T(8,128)S(1)} %copy.7.ids_ref, bf16[16,8192]{1,0:T(8,128)(2,1)S(1)} %copy-done.1, s32[2,128]{1,0:T(2,128)S(1)} %copy-done.3, bf16[2,1024,1024]{2,1,0:T(8,128)(2,1)S(1)} %copy-done, bf16[512,8192]{1,0:T(8,128)(2,1)} %w_hbm.1), custom_call_target="tpu_custom_call" | custom-call | tf_op jit(solution)/shard_map/pallas_call | solution.py:415
  96.6 0.7 copy.9
Async XLA Ops:
  0.7 2.2 %copy-start = (bf16[2,1024,1024]{2,1,0:T(8,128)(2,1)S(1)}, bf16[2,1024,1024]{2,1,0:T(8,128)(2,1)}, u32[]{:S(2)}) copy-start(bf16[2,1024,1024]{2,1,0:T(8,128)(2,1)} %kv_hbm.1) | copy-start | bytes 12582916
  2.9 0.9 copy-start.1
  3.9 0.9 copy-start.2
  4.8 0.7 copy-start.3

commit v2 on v1

--- a/solution.py
+++ b/solution.py
@@ -121,11 +121,15 @@
 
 
 def fused_kernel(
-    q_ref, ids_ref, table_ref, blocks_ref, kv_hbm, w_hbm, out_ref,
-    kv_ref, w_ref, q_all, bias_ref, q_rows, v_t,
-    o_loc, s_loc, r1, rs1, t1, ts1, r2, rs2, t2, ts2, r3, rs3, t3, ts3, r4, rs4,
-    att, p0, pr1, p1, pr2, p2, pr3, p3, pr4,
-    kv_sem, w_sem, ag_send, ag_recv, rs_send, rs_recv, ss_send, ss_recv, pj_send, pj_recv,
+    q_ref, ids_hbm, table_hbm, blocks_hbm, kv_hbm, w_hbm, out_ref,
+    ids_ref, table_ref, blocks_ref, kv_ref, w_ref, q_all, bias_ref, q_rows, v_t,
+    o_send, s_send, o_keep, s_keep, r1, rs1,
+    t1s, ts1s, t1k, ts1k, r2, rs2,
+    t2s, ts2s, t2k, ts2k, r3, rs3,
+    t3s, ts3s, t3k, ts3k, r4, rs4,
+    att, p0, p0s, pr1, p1, p1s, pr2, p2, p2s, pr3, p3, p3s, pr4,
+    ids_sem, table_sem, blocks_sem, kv_sem, w_sem,
+    ag_send, ag_recv, rs_send, rs_recv, ss_send, ss_recv, pj_send, pj_recv,
 ):
     me = lax.axis_index("ctx")
     core = me % 2
@@ -144,15 +148,25 @@
 
     kv_load = pltpu.make_async_copy(kv_hbm, kv_ref, kv_sem)
     w_load = pltpu.make_async_copy(w_hbm, w_ref, w_sem)
-    kv_load.start()
-    w_load.start()
+    ids_load = pltpu.make_async_copy(ids_hbm, ids_ref, ids_sem)
+    table_load = pltpu.make_async_copy(table_hbm, table_ref, table_sem)
+    blocks_load = pltpu.make_async_copy(blocks_hbm, blocks_ref, blocks_sem)
+    for load in (ids_load, table_load, blocks_load, kv_load, w_load):
+        load.start()
 
     barrier = pltpu.get_barrier_semaphore()
     for other in (to_core, to_y, to_z0, to_z1):
         pl.semaphore_signal(barrier, inc=1, device_id={"ctx": other}, device_id_type=MESH)
 
+    ids_load.wait()
+    table_load.wait()
+    blocks_load.wait()
+    row_at = lax.broadcasted_iota(jnp.int32, (rows, rows), 0)
+    lane_at = lax.broadcasted_iota(jnp.int32, (rows, rows), 1)
+    ids_wide = jnp.broadcast_to(ids_ref[...].astype(jnp.float32), (rows, rows))
+    ids_col = jnp.sum(jnp.where(row_at == lane_at, ids_wide, 0.0), axis=1, keepdims=True)
     lookup_ids = lax.broadcasted_iota(jnp.int32, (rows, table_ref.shape[0]), 1)
-    one_hot = jnp.where(ids_ref[...] == lookup_ids, 1.0, 0.0).astype(jnp.bfloat16)
+    one_hot = jnp.where(ids_col == lookup_ids.astype(jnp.float32), 1.0, 0.0).astype(jnp.bfloat16)
     for g in range(groups):
         cols = slice(g * GROUP * HEAD, (g + 1) * GROUP * HEAD)
         lookup = jnp.dot(one_hot, table_ref[:, cols], preferred_element_type=jnp.float32)
@@ -179,19 +193,24 @@
             ref, other = q_all.at[g, :, :, :, core], to_core
         return remote(ref, ref, ag_send.at[step, g], ag_recv.at[step, g], other)
 
+    def pick(mine, bit):
+        return mine * bit + (1 - mine) * (1 - bit)
+
+    def order(step, p):
+        a = z1 if step >= 1 else 1 - z1
+        b = z0 if step >= 2 else 1 - z0
+        c = y if step >= 3 else 1 - y
+        return 4 * pick(a, p // 4) + 2 * pick(b, (p // 2) % 2) + pick(c, p % 2)
+
     def merge_copies(step, i):
         if step == 0:
-            a, b = (o_loc.at[i, 1 - core], r1.at[i]), (s_loc.at[i, 1 - core], rs1.at[i])
-            other = to_core
+            a, b, other = (o_send.at[i], r1.at[i]), (s_send.at[i], rs1.at[i]), to_core
         elif step == 1:
-            a, b = (t1.at[2 * i + 1 - y], r2.at[i]), (ts1.at[2 * i + 1 - y], rs2.at[i])
-            other = to_y
+            a, b, other = (t1s.at[i], r2.at[i]), (ts1s.at[i], rs2.at[i]), to_y
         elif step == 2:
-            a, b = (t2.at[2 * i + 1 - z0], r3.at[i]), (ts2.at[2 * i + 1 - z0], rs3.at[i])
-            other = to_z0
+            a, b, other = (t2s.at[i], r3.at[i]), (ts2s.at[i], rs3.at[i]), to_z0
         else:
-            a, b = (t3.at[1 - z1], r4.at[i]), (ts3.at[1 - z1], rs4.at[i])
-            other = to_z1
+            a, b, other = (t3s.at[i], r4.at[i]), (ts3s.at[i], rs4.at[i]), to_z1
         return (
             remote(a[0], a[1], rs_send.at[step, i], rs_recv.at[step, i], other),
             remote(b[0], b[1], ss_send.at[step, i], ss_recv.at[step, i], other),
@@ -219,7 +238,7 @@
             o_dst[h] = (
                 oa[h].astype(jnp.float32) * wa[h:h + 1]
                 + ob[h].astype(jnp.float32) * wb[h:h + 1]
-            ).astype(jnp.bfloat16)
+            ).astype(o_dst.dtype)
 
     first = me * key_blocks
     block_ids = first + lax.broadcasted_iota(jnp.int32, (key_blocks, blocks_ref.shape[1]), 0)
@@ -234,8 +253,8 @@
     pl.semaphore_wait(barrier, 4)
 
     @pl.loop(0, groups)
-    def _(g):
-        gather(0, g).start()
+    def _(p):
+        gather(0, order(0, p)).start()
 
     kv_load.wait()
 
@@ -247,114 +266,137 @@
             head_rows = q_wide[:, h * rows:(h + 1) * rows, :].reshape(queries, HEAD)
             q_rows[h // 2, (h % 2) * queries:(h % 2 + 1) * queries] = head_rows.astype(jnp.bfloat16)
 
-        @pl.loop(0, GROUP // 2)
-        def _(hp):
-            scores = lax.dot_general(
-                kv_ref[0, :, lanes], q_rows[hp], (((1,), (1,)), ((), ())),
-                preferred_element_type=jnp.float32,
-            )
-            scores = scores.reshape(key_blocks, BLOCK, 2 * queries) + bias_ref[...][:, None, :]
-            scores = scores.reshape(keys, 2 * queries)
-            peak = jnp.max(scores, axis=0, keepdims=True)
-            weights = jnp.exp2((scores - peak) * EXP_SCALE)
-            total = jnp.sum(weights, axis=0, keepdims=True)
-            part = jnp.dot(v_t[...], weights.astype(jnp.bfloat16), preferred_element_type=jnp.float32)
-            half = hp // (OWN // 2)
-            base = (hp % (OWN // 2)) * 2
-            for i in range(2):
-                lane = slice(i * queries, (i + 1) * queries)
-                o_loc[g, half, base + i] = part[:, lane].astype(jnp.bfloat16)
-                s_loc[g, half, pl.ds(base + i, 1), :] = peak[:, lane]
-                s_loc[g, half, pl.ds(OWN + base + i, 1), :] = total[:, lane]
+        def heads(half, o_dst, s_dst):
+            @pl.loop(0, OWN // 2)
+            def _(i):
+                scores = lax.dot_general(
+                    kv_ref[0, :, lanes], q_rows[half * (OWN // 2) + i], (((1,), (1,)), ((), ())),
+                    preferred_element_type=jnp.float32,
+                )
+                scores = scores.reshape(key_blocks, BLOCK, 2 * queries) + bias_ref[...][:, None, :]
+                scores = scores.reshape(keys, 2 * queries)
+                peak = jnp.max(scores, axis=0, keepdims=True)
+                weights = jnp.exp2((scores - peak) * EXP_SCALE)
+                total = jnp.sum(weights, axis=0, keepdims=True)
+                part = jnp.dot(v_t[...], weights.astype(jnp.bfloat16), preferred_element_type=jnp.float32)
+                for h in range(2):
+                    lane = slice(h * queries, (h + 1) * queries)
+                    o_dst[g, 2 * i + h] = part[:, lane].astype(o_dst.dtype)
+                    s_dst[g, pl.ds(2 * i + h, 1), :] = peak[:, lane]
+                    s_dst[g, pl.ds(OWN + 2 * i + h, 1), :] = total[:, lane]
+
+        heads(1 - core, o_send, s_send)
+        start_merge(0, g)
+        heads(core, o_keep, s_keep)
 
     def at(cond, fn):
         pl.when(cond)(fn)
 
-    @pl.loop(0, groups + 6)
+    @pl.loop(0, groups + 9)
     def _(t):
         for step in range(3):
             def advance(step=step):
-                gather(step, t - step).wait_recv()
-                gather(step + 1, t - step).start()
-            at((t >= step) & (t < groups + step), advance)
+                g = order(step + 1, t - 2 * step)
+                gather(step, g).wait_recv()
+                gather(step + 1, g).start()
+            at((t >= 2 * step) & (t < groups + 2 * step), advance)
 
         def attention():
-            g = t - 3
+            g = order(3, t - 6)
             gather(3, g).wait_recv()
             attend(g)
-            start_merge(0, g)
-        at((t >= 3) & (t < groups + 3), attention)
+        at((t >= 6) & (t < groups + 6), attention)
 
         def merge_core():
-            g = t - 4
+            p = t - 7
+            g = order(3, p)
+            j = g // 2
             wait_merge(0, g)
-            merge(o_loc.at[g, core], s_loc.at[g, core], r1.at[g], rs1.at[g], t1.at[g], ts1.at[g])
-            at(g % 2 == 1, lambda: start_merge(1, g // 2))
-        at((t >= 4) & (t < groups + 4), merge_core)
+            parts = (o_keep.at[g], s_keep.at[g], r1.at[g], rs1.at[g])
+
+            def send():
+                merge(*parts, t1s.at[j], ts1s.at[j])
+                start_merge(1, j)
+            at(p % 2 == 0, send)
+            at(p % 2 == 1, lambda: merge(*parts, t1k.at[j], ts1k.at[j]))
+        at((t >= 7) & (t < groups + 7), merge_core)
 
         def merge_y():
-            j = (t - 5) // 2
+            p = t - 8
+            j = order(3, p) // 2
+            k = j // 2
             wait_merge(1, j)
-            merge(t1.at[2 * j + y], ts1.at[2 * j + y], r2.at[j], rs2.at[j], t2.at[j], ts2.at[j])
-            at(j % 2 == 1, lambda: start_merge(2, j // 2))
-        at((t >= 6) & (t < groups + 5) & (t % 2 == 0), merge_y)
+            parts = (t1k.at[j], ts1k.at[j], r2.at[j], rs2.at[j])
+
+            def send():
+                merge(*parts, t2s.at[k], ts2s.at[k])
+                start_merge(2, k)
+            at(p % 4 == 1, send)
+            at(p % 4 == 3, lambda: merge(*parts, t2k.at[k], ts2k.at[k]))
+        at((t >= 9) & (t < groups + 8) & (t % 2 == 1), merge_y)
 
         def merge_z0():
-            k = (t - 6) // 4
+            p = t - 9
+            k = order(3, p) // 4
             wait_merge(2, k)
-            merge(t2.at[2 * k + z0], ts2.at[2 * k + z0], r3.at[k], rs3.at[k], t3.at[k], ts3.at[k])
-        at((t >= 9) & (t < groups + 6) & (t % 4 == 1), merge_z0)
-
-    start_merge(3, 0)
+            parts = (t2k.at[k], ts2k.at[k], r3.at[k], rs3.at[k])
+
+            def send():
+                merge(*parts, t3s.at[0], ts3s.at[0])
+                start_merge(3, 0)
+            at(p == 3, send)
+            at(p == 7, lambda: merge(*parts, t3k.at[0], ts3k.at[0]))
+        at((t == 12) | (t == 16), merge_z0)
+
     w_load.wait()
     wait_merge(3, 0)
-    peak, wa, wb, total = merge_stats(ts3[z1], rs4[0])
+    peak, wa, wb, total = merge_stats(ts3k[0], rs4[0])
     inverse = 1.0 / total
     wa, wb = wa * inverse, wb * inverse
     for h in range(OWN):
-        done = t3[z1, h].astype(jnp.float32) * wa[h:h + 1] + r4[0, h].astype(jnp.float32) * wb[h:h + 1]
+        done = t3k[0, h] * wa[h:h + 1] + r4[0, h].astype(jnp.float32) * wb[h:h + 1]
         att[:, h * HEAD:(h + 1) * HEAD] = done.T.astype(jnp.bfloat16)
 
     def project_copy(step, c):
         swap = c % 2 == 1
         if step == 0:
-            src, dst, other = p0.at[c, :, :, :, 1 - core], pr1.at[c], to_core
+            src, dst, other = p0s.at[c], pr1.at[c], to_core
         elif step == 1:
-            src = p1.at[c, :, 1 - z0] if swap else p1.at[c, :, :, 1 - y]
-            dst, other = pr2.at[c], to_z0 if swap else to_y
+            src, dst, other = p1s.at[c], pr2.at[c], to_z0 if swap else to_y
         elif step == 2:
-            src = p2.at[c, :, 1 - y] if swap else p2.at[c, :, 1 - z0]
-            dst, other = pr3.at[c], to_y if swap else to_z0
+            src, dst, other = p2s.at[c], pr3.at[c], to_y if swap else to_z0
         else:
-            src, dst, other = p3.at[c, 1 - z1], pr4.at[c], to_z1
+            src, dst, other = p3s.at[c], pr4.at[c], to_z1
         return remote(src, dst, pj_send.at[step, c], pj_recv.at[step, c], other)
-
-    def add(a, b):
-        return (a.astype(jnp.float32) + b.astype(jnp.float32)).astype(jnp.bfloat16)
 
     def stage(step, c):
         swap = c % 2 == 1
+        low = jnp.bfloat16
+        if step > 0:
+            project_copy(step - 1, c).wait_recv()
         if step == 0:
             halves = []
             for i in range(2):
                 base = c * CHUNK_COLS + i * TILE
                 part = jnp.dot(att[...], w_ref[:, base:base + TILE], preferred_element_type=jnp.float32)
                 halves.append(part.reshape(2 * groups, rows, TILE))
-            both = jnp.concatenate(halves, axis=1).astype(jnp.bfloat16)
+            both = jnp.concatenate(halves, axis=1)
             p0[c] = both.reshape(2, 2, 2, 2, 2 * rows, TILE)
+            p0s[c] = p0[c, :, :, :, 1 - core].astype(low)
+        elif step == 1:
+            p1[c] = p0[c, :, :, :, core] + pr1[c].astype(jnp.float32)
+            p1s[c] = (p1[c, :, 1 - z0] if swap else p1[c, :, :, 1 - y]).astype(low)
+        elif step == 2:
+            p2[c] = (p1[c, :, z0] if swap else p1[c, :, :, y]) + pr2[c].astype(jnp.float32)
+            p2s[c] = (p2[c, :, 1 - y] if swap else p2[c, :, 1 - z0]).astype(low)
+        elif step == 3:
+            p3[c] = (p2[c, :, y] if swap else p2[c, :, z0]) + pr3[c].astype(jnp.float32)
+            p3s[c] = p3[c, 1 - z1].astype(low)
         else:
-            project_copy(step - 1, c).wait_recv()
-            if step == 1:
-                p1[c] = add(p0[c, :, :, :, core], pr1[c])
-            elif step == 2:
-                p2[c] = add(p1[c, :, z0] if swap else p1[c, :, :, y], pr2[c])
-            elif step == 3:
-                p3[c] = add(p2[c, :, y] if swap else p2[c, :, z0], pr3[c])
-            else:
-                done = p3[c, z1].astype(jnp.float32) + pr4[c].astype(jnp.float32)
-                for i in range(2):
-                    base = c * CHUNK_COLS + i * TILE
-                    out_ref[:, base:base + TILE] = done[i * rows:(i + 1) * rows].astype(jnp.bfloat16)
+            done = p3[c, z1] + pr4[c].astype(jnp.float32)
+            for i in range(2):
+                base = c * CHUNK_COLS + i * TILE
+                out_ref[:, base:base + TILE] = done[i * rows:(i + 1) * rows].astype(low)
         if step < 4:
             project_copy(step, c).start()
 
@@ -369,7 +411,7 @@
             gather(step, g).wait_send()
 
     for step in range(4):
-        for i in range(groups >> step):
+        for i in range(max(groups >> step, 1)):
             for copy in merge_copies(step, i):
                 copy.wait_send()
         for c in range(CHUNKS):
@@ -386,42 +428,38 @@
     stat = (2 * OWN, total_q)
     tile = (2 * rows, TILE)
     scratch = [
+        pltpu.VMEM((1, rows), jnp.int32),
+        pltpu.VMEM(steer_table.shape, bf),
+        pltpu.VMEM(blocks.shape, jnp.int32),
         pltpu.VMEM(kv.shape, bf),
         pltpu.VMEM(w_out.shape, bf),
         pltpu.VMEM((groups, 2, 2, 2, 2, GROUP * rows, HEAD), bf),
         pltpu.VMEM((keys // BLOCK, 2 * total_q), f32),
         pltpu.VMEM((GROUP // 2, 2 * total_q, HEAD), bf),
         pltpu.VMEM((HEAD, keys), bf),
-        pltpu.VMEM((groups, 2) + piece, bf),
-        pltpu.VMEM((groups, 2) + stat, f32),
     ]
-    for count in (groups, groups // 2, groups // 4):
-        scratch += [
-            pltpu.VMEM((count,) + piece, bf), pltpu.VMEM((count,) + stat, f32),
-            pltpu.VMEM((count,) + piece, bf), pltpu.VMEM((count,) + stat, f32),
-        ]
-    scratch += [pltpu.VMEM((1,) + piece, bf), pltpu.VMEM((1,) + stat, f32)]
-    scratch += [
-        pltpu.VMEM((total_q, OWN * HEAD), bf),
-        pltpu.VMEM((CHUNKS, 2, 2, 2, 2) + tile, bf),
-    ]
+    for count in (groups, groups // 2, groups // 4, groups // 8):
+        for kind in (bf, f32, bf):
+            scratch += [pltpu.VMEM((count,) + piece, kind), pltpu.VMEM((count,) + stat, f32)]
+    scratch += [pltpu.VMEM((total_q, OWN * HEAD), bf), pltpu.VMEM((CHUNKS, 2, 2, 2, 2) + tile, f32)]
     for lead in ((2, 2, 2), (2, 2), (2,)):
-        scratch += [pltpu.VMEM((CHUNKS,) + lead + tile, bf), pltpu.VMEM((CHUNKS,) + lead + tile, bf)]
-    scratch += [pltpu.VMEM((CHUNKS,) + tile, bf)]
+        many = (CHUNKS,) + lead + tile
+        scratch += [pltpu.VMEM(many, bf), pltpu.VMEM(many, bf), pltpu.VMEM(many, f32)]
+    scratch += [pltpu.VMEM((CHUNKS,) + tile, bf), pltpu.VMEM((CHUNKS,) + tile, bf)]
     dma = pltpu.SemaphoreType.DMA
-    scratch += [dma(()), dma(())] + [dma((4, groups))] * 6 + [dma((4, CHUNKS))] * 2
+    scratch += [dma(())] * 5 + [dma((4, groups))] * 6 + [dma((4, CHUNKS))] * 2
     vmem = pl.BlockSpec(memory_space=pltpu.VMEM)
     hbm = pl.BlockSpec(memory_space=pl.ANY)
     return pl.pallas_call(
         fused_kernel,
         out_shape=jax.ShapeDtypeStruct(queries.shape, bf),
-        in_specs=[vmem, vmem, vmem, vmem, hbm, hbm],
+        in_specs=[vmem, hbm, hbm, hbm, hbm, hbm],
         out_specs=vmem,
         scratch_shapes=scratch,
         compiler_params=pltpu.CompilerParams(
             collective_id=0, has_side_effects=True, vmem_limit_bytes=48 * 1024 * 1024
         ),
-    )(queries, steer_ids[:, None], steer_table, blocks, kv, w_out)
+    )(queries, steer_ids[None, :], steer_table, blocks, kv, w_out)
 
 
 def solution(mesh):

time: 97.9 us -> 83.6 us (0.85)
  Pallas kernels: 91.2 us -> 77.3 us
    pallas_call x1, Pallas kernels: 91.2 us -> 77.3 us  [per_device_fused(): pl.pallas_call(fused_kernel, out_shape=jax.ShapeDtypeStruct(queries.shape...]
    unnamed x9 -> x11, local copies, waits for them, and re-layouts: 5.38 us -> 6.03 us
where the time goes in v2:
time: 83.6 us; the launch traced here: 83.4 us
  Pallas kernels  77.3 us (92%)
  local copies, waits for them, and re-layouts  6.03 us (7%)
    pallas_call x1, Pallas kernels, per_device_fused(): pl.pallas_call(fused_kernel, out_shape=jax.ShapeDtypeStruct(queries.shape...  77.3 us
    unnamed x11, local copies, waits for them, and re-layouts  6.03 us

profile of v2, /device:TPU:0, one launch (start us, length us, event | category | flops | bytes accessed | tf_op | source)
XLA Modules:
  0.0 83.4 jit_solution(8507670617139663331)
XLA Ops:
  0.0 0.0 copy-start
  0.0 2.2 %copy-done = bf16[2,1024,1024]{2,1,0:T(8,128)(2,1)S(1)} copy-done((bf16[2,1024,1024]{2,1,0:T(8,128)(2,1)S(1)}, bf16[2,1024,1024]{2,1,0:T(8,128)(2,1)}, u32[]{:S(2)}) %copy-start) | copy-done | bytes 4194328
  2.2 0.0 copy-start.1
  2.2 0.9 %copy-done.1 = bf16[16,8192]{1,0:T(8,128)(2,1)S(1)} copy-done((bf16[16,8192]{1,0:T(8,128)(2,1)S(1)}, bf16[16,8192]{1,0:T(8,128)(2,1)}, u32[]{:S(2)}) %copy-start.1) | copy-done | bytes 262168
  3.1 0.0 copy-start.2
  3.1 0.9 %copy-done.2 = bf16[8,8192]{1,0:T(8,128)(2,1)S(1)} copy-done((bf16[8,8192]{1,0:T(8,128)(2,1)S(1)}, bf16[8,8192]{1,0:T(8,128)(2,1)}, u32[]{:S(2)}) %copy-start.2) | copy-done | bytes 131096
  4.0 0.0 copy-start.3
  4.0 0.7 copy-done.3
  4.7 0.0 copy-start.4
  4.7 0.7 copy-done.4
  5.4 77.3 %shard_map.64 = bf16[8,8192]{1,0:T(8,128)(2,1)S(1)} custom-call(bf16[8,8192]{1,0:T(8,128)(2,1)S(1)} %copy-done.2, s32[1,8]{1,0:T(1,128)S(1)} %bitcast.1, bf16[16,8192]{1,0:T(8,128)(2,1)S(1)} %copy-done.1, s32[2,128]{1,0:T(2,128)S(1)} %copy-done.3, bf16[2,1024,1024]{2,1,0:T(8,128)(2,1)S(1)} %copy-done, bf16[512,8192]{1,0:T(8,128)(2,1)} %w_hbm.1), custom_call_target="tpu_custom_call" | custom-call | tf_op jit(solution)/shard_map/pallas_call | solution.py:453
  82.7 0.7 copy.8
Async XLA Ops:
  0.0 2.2 %copy-start = (bf16[2,1024,1024]{2,1,0:T(8,128)(2,1)S(1)}, bf16[2,1024,1024]{2,1,0:T(8,128)(2,1)}, u32[]{:S(2)}) copy-start(bf16[2,1024,1024]{2,1,0:T(8,128)(2,1)} %kv_hbm.1) | copy-start | bytes 12582916
  2.2 0.9 %copy-start.1 = (bf16[16,8192]{1,0:T(8,128)(2,1)S(1)}, bf16[16,8192]{1,0:T(8,128)(2,1)}, u32[]{:S(2)}) copy-start(bf16[16,8192]{1,0:T(8,128)(2,1)} %table_hbm.1) | copy-start | bytes 786436
  3.1 0.9 %copy-start.2 = (bf16[8,8192]{1,0:T(8,128)(2,1)S(1)}, bf16[8,8192]{1,0:T(8,128)(2,1)}, u32[]{:S(2)}) copy-start(bf16[8,8192]{1,0:T(8,128)(2,1)} %q_ref.1) | copy-start | bytes 393220
  4.0 0.7 copy-start.3
  4.7 0.7 copy-start.4

commit v3 on v2

--- a/solution.py
+++ b/solution.py
@@ -256,8 +256,6 @@
     def _(p):
         gather(0, order(0, p)).start()
 
-    kv_load.wait()
-
     def attend(g):
         lanes = pl.ds(pl.multiple_of(g * HEAD, HEAD), HEAD)
         v_t[...] = kv_ref[1, :, lanes].T
@@ -301,12 +299,6 @@
                 gather(step + 1, g).start()
             at((t >= 2 * step) & (t < groups + 2 * step), advance)
 
-        def attention():
-            g = order(3, t - 6)
-            gather(3, g).wait_recv()
-            attend(g)
-        at((t >= 6) & (t < groups + 6), attention)
-
         def merge_core():
             p = t - 7
             g = order(3, p)
@@ -347,6 +339,13 @@
             at(p == 3, send)
             at(p == 7, lambda: merge(*parts, t3k.at[0], ts3k.at[0]))
         at((t == 12) | (t == 16), merge_z0)
+
+        def attention():
+            g = order(3, t - 6)
+            gather(3, g).wait_recv()
+            at(t == 6, kv_load.wait)
+            attend(g)
+        at((t >= 6) & (t < groups + 6), attention)
 
     w_load.wait()
     wait_merge(3, 0)
@@ -400,10 +399,9 @@
         if step < 4:
             project_copy(step, c).start()
 
-    for t in range(CHUNKS + 4):
-        for step in range(5):
-            if 0 <= t - step < CHUNKS:
-                stage(step, t - step)
+    for step in range(5):
+        for c in range(CHUNKS):
+            stage(step, c)
 
     @pl.loop(0, groups)
     def _(g):

time: 83.6 us -> 77.8 us (0.931)
  Pallas kernels: 77.3 us -> 71.5 us
    pallas_call x1, Pallas kernels: 77.3 us -> 71.5 us  [per_device_fused(): pl.pallas_call(fused_kernel, out_shape=jax.ShapeDtypeStruct(queries.shape...]
where the time goes in v3:
time: 77.8 us; the launch traced here: 77.6 us
  Pallas kernels  71.5 us (92%)
  local copies, waits for them, and re-layouts  6.03 us (8%)
    pallas_call x1, Pallas kernels, per_device_fused(): pl.pallas_call(fused_kernel, out_shape=jax.ShapeDtypeStruct(queries.shape...  71.5 us
    unnamed x11, local copies, waits for them, and re-layouts  6.03 us

profile of v3, /device:TPU:0, one launch (start us, length us, event | category | flops | bytes accessed | tf_op | source)
XLA Modules:
  0.0 77.6 jit_solution(6794852506456090295)
XLA Ops:
  0.0 0.0 copy-start
  0.0 2.2 %copy-done = bf16[2,1024,1024]{2,1,0:T(8,128)(2,1)S(1)} copy-done((bf16[2,1024,1024]{2,1,0:T(8,128)(2,1)S(1)}, bf16[2,1024,1024]{2,1,0:T(8,128)(2,1)}, u32[]{:S(2)}) %copy-start) | copy-done | bytes 4194328
  2.2 0.0 copy-start.1
  2.2 0.9 %copy-done.1 = bf16[16,8192]{1,0:T(8,128)(2,1)S(1)} copy-done((bf16[16,8192]{1,0:T(8,128)(2,1)S(1)}, bf16[16,8192]{1,0:T(8,128)(2,1)}, u32[]{:S(2)}) %copy-start.1) | copy-done | bytes 262168
  3.1 0.0 copy-start.2
  3.1 0.9 %copy-done.2 = bf16[8,8192]{1,0:T(8,128)(2,1)S(1)} copy-done((bf16[8,8192]{1,0:T(8,128)(2,1)S(1)}, bf16[8,8192]{1,0:T(8,128)(2,1)}, u32[]{:S(2)}) %copy-start.2) | copy-done | bytes 131096
  4.0 0.0 copy-start.3
  4.0 0.7 copy-done.3
  4.7 0.0 copy-start.4
  4.7 0.7 copy-done.4
  5.4 71.5 %shard_map.64 = bf16[8,8192]{1,0:T(8,128)(2,1)S(1)} custom-call(bf16[8,8192]{1,0:T(8,128)(2,1)S(1)} %copy-done.2, s32[1,8]{1,0:T(1,128)S(1)} %bitcast.1, bf16[16,8192]{1,0:T(8,128)(2,1)S(1)} %copy-done.1, s32[2,128]{1,0:T(2,128)S(1)} %copy-done.3, bf16[2,1024,1024]{2,1,0:T(8,128)(2,1)S(1)} %copy-done, bf16[512,8192]{1,0:T(8,128)(2,1)} %w_hbm.1), custom_call_target="tpu_custom_call" | custom-call | tf_op jit(solution)/shard_map/pallas_call | solution.py:451
  76.9 0.7 copy.8
Async XLA Ops:
  0.0 2.2 %copy-start = (bf16[2,1024,1024]{2,1,0:T(8,128)(2,1)S(1)}, bf16[2,1024,1024]{2,1,0:T(8,128)(2,1)}, u32[]{:S(2)}) copy-start(bf16[2,1024,1024]{2,1,0:T(8,128)(2,1)} %kv_hbm.1) | copy-start | bytes 12582916
  2.2 0.9 %copy-start.1 = (bf16[16,8192]{1,0:T(8,128)(2,1)S(1)}, bf16[16,8192]{1,0:T(8,128)(2,1)}, u32[]{:S(2)}) copy-start(bf16[16,8192]{1,0:T(8,128)(2,1)} %table_hbm.1) | copy-start | bytes 786436
  3.1 0.9 %copy-start.2 = (bf16[8,8192]{1,0:T(8,128)(2,1)S(1)}, bf16[8,8192]{1,0:T(8,128)(2,1)}, u32[]{:S(2)}) copy-start(bf16[8,8192]{1,0:T(8,128)(2,1)} %q_ref.1) | copy-start | bytes 393220
  4.0 0.7 copy-start.3
  4.7 0.7 copy-start.4
